TPU v7x, 32 devices: a whole 2x2x4 slice. The times are simulated.
32 devices in a mesh: member: 4 (over y, x), space: 8 (over z, core).
Axes of the slice: x: 2, y: 2, z: 4, core: 2. Of those that a mesh axis runs over, the one named last changes fastest.
Arguments:
- zonal_wind: bfloat16 [24, 64, 256, 128], P('member', 'space'), may hold values from -6 to 6
- meridional_wind: bfloat16 [24, 64, 256, 128], P('member', 'space'), may hold values from -6 to 6
- heat_anomaly: bfloat16 [24, 64, 256, 128], P('member', 'space'), may hold values from -6 to 6
- moisture_anomaly: bfloat16 [24, 64, 256, 128], P('member', 'space'), may hold values from -6 to 6
- projection_scale: float32 [64, 256], P('space'), may hold values from 0.5 to 2
- balance_multiplier: float32 [64, 256], P('space'), may hold values from -4 to 4
- heat_on_curl_slope: float32 [128], replicated, may hold values from 0.3 to 1.5
- moisture_on_heat_slope: float32 [128], replicated, may hold values from 0.3 to 1.5
Outputs:
- covariance: float32 [8, 512, 512], P('space', 'member')
All inputs are finite; a program needn't handle non-finite values.
Results may differ from a plain program's by a relative error of at most 0.0009.
Values may be sent and summed in bfloat16 or wider, within the bound.
A program may use at most 128 MiB of HBM per device.

v0:
```python
import jax
import jax.numpy as jnp
from jax import lax
from jax.sharding import PartitionSpec as P


def extended(block, sides, width):
    for axis, dim in sides:
        count = lax.axis_size(axis)
        forward = [(i, i + 1) for i in range(count - 1)]
        backward = [(target, source) for source, target in forward]
        low = lax.ppermute(
            lax.slice_in_dim(block, block.shape[dim] - width, None, axis=dim), axis, forward
        )
        high = lax.ppermute(lax.slice_in_dim(block, 0, width, axis=dim), axis, backward)
        block = jnp.concatenate([low, block, high], axis=dim)
    return block


def lat_diff(padded):
    return (-padded[:, 4:] + 8.0 * padded[:, 3:-1] - 8.0 * padded[:, 1:-3] + padded[:, :-4]) / 12.0


def lon_diff(field):
    return (jnp.roll(field, -1, 2) - jnp.roll(field, 1, 2)) / 2.0


def gram_rows(left, right, precision):
    return lax.dot_general(
        left,
        right,
        (((0,), (0,)), ((), ())),
        preferred_element_type=jnp.float32,
        precision=precision,
    )


def on_device(
    zonal_wind,
    meridional_wind,
    heat_anomaly,
    moisture_anomaly,
    projection_scale,
    balance_multiplier,
    heat_on_curl_slope,
    moisture_on_heat_slope,
):
    winds = jnp.stack([zonal_wind, meridional_wind])
    padded = extended(winds, (("space", 2),), 2)
    u_full = padded[0].astype(jnp.float32)
    v_full = padded[1].astype(jnp.float32)
    u_mid = u_full[:, 2:-2]
    v_mid = v_full[:, 2:-2]
    factor = projection_scale[None, :, :, None]
    wind_curl = factor * (lon_diff(v_mid) - lat_diff(u_full))
    wind_spreading = factor * (lon_diff(u_mid) + lat_diff(v_full))
    heat_residual = (
        heat_anomaly.astype(jnp.float32)
        - heat_on_curl_slope * balance_multiplier[None, :, :, None] * wind_curl
    )
    moisture_residual = (
        moisture_anomaly.astype(jnp.float32) - moisture_on_heat_slope * heat_residual
    )
    sample_vector = jnp.concatenate(
        [wind_curl, wind_spreading, heat_residual, moisture_residual], axis=3
    ).astype(jnp.bfloat16)
    width = sample_vector.shape[3]
    groups = lax.axis_size("member")
    members_all = float(sample_vector.shape[0] * groups)
    rows = width // groups
    scale = 1.0 / (
        (sample_vector.shape[0] * groups - 1) * sample_vector.shape[1] * sample_vector.shape[2]
    )
    local_sum = jnp.sum(sample_vector.astype(jnp.float32), axis=0)
    highest = lax.Precision.HIGHEST
    totals = lax.psum(local_sum.astype(jnp.bfloat16), "member").astype(jnp.float32)
    ens_mean = totals / members_all
    anomaly = (sample_vector.astype(jnp.float32) - ens_mean[None]).reshape(-1, width)
    summed = lax.psum(gram_rows(anomaly, anomaly, highest), "member")
    mine = lax.dynamic_slice_in_dim(summed, lax.axis_index("member") * rows, rows, 0)
    return (mine * scale)[None]


def solution(mesh):
    placed = (
        P("member", "space", None, None),
        P("member", "space", None, None),
        P("member", "space", None, None),
        P("member", "space", None, None),
        P("space", None),
        P("space", None),
        P(),
        P(),
    )
    return jax.shard_map(
        on_device, mesh=mesh, in_specs=placed, out_specs=P("space", "member", None), check_vma=False
    )
```

profile of v0, /device:TPU:0, one launch (start us, length us, event | category | flops | bytes accessed | tf_op | source)
XLA Modules:
  0.0 297.9 jit_solution(10177607277210640226)
XLA Ops:
  6.5 0.0 copy-start.4
  6.5 0.0 copy-start.7
  6.5 0.0 copy-start.9
  6.5 0.0 all-reduce.3.cloned.1.call-start
  6.5 0.0 copy-start.5
  6.5 2.3 pad_maximum_fusion.4
  8.8 2.6 collective-permute-start
  11.4 1.3 collective-permute-start.1
  12.7 0.0 copy-done.7
  12.7 0.0 copy-done.9
  12.7 1.3 broadcast_multiply_fusion
  14.1 0.2 collective-permute-done
  14.3 4.5 %collective-permute-done.1 = bf16[2,6,2,256,128]{4,3,2,1,0:T(8,128)(2,1)S(1)} collective-permute-done((bf16[2,6,2,256,128]{4,3,2,1,0:T(8,128)(2,1)S(1)}, bf16[2,6,2,256,128]{4,3,2,1,0:T(8,128)(2,1)S(1)}, u32[]{:S(2)}, u32[]{:S(2)}) %collective-permute-start.1) | collective-permute-done | bytes 1572896 | tf_op jit(solution)/shard_map/ppermute | solution.py:15
  18.8 0.0 copy-done.4
  18.8 0.0 copy-done.5
  18.8 4.4 %pad_maximum_fusion.1 = bf16[2,6,12,256,128]{4,3,2,1,0:T(8,128)(2,1)} fusion(bf16[2,6,2,256,128]{4,3,2,1,0:T(8,128)(2,1)S(1)} %collective-permute-done.1, bf16[1,6,8,256,128]{4,3,2,1,0:T(8,128)(2,1)S(1)} %bitcast.21, bf16[1,6,8,256,128]{4,3,2,1,0:T(8,128)(2,1)S(1)} %bitcast.23, bf16[2,6,2,256,128]{4,3,2,1,0:T(8,128)(2,1)S(1)} %collective-permute-done), kind=kLoop, calls=%fused_computation.5 | loop fusion | flops 14155776 | bytes 18874368 | tf_op jit(solution)/shard_map/concatenate | solution.py:16
  23.2 12.8 %fusion.18 = (f32[6,12,256,128]{3,2,1,0:T(8,128)}, f32[6,12,256,128]{3,2,1,0:T(8,128)}) fusion(bf16[2,6,12,256,128]{4,3,2,1,0:T(8,128)(2,1)} %pad_maximum_fusion.1), kind=kLoop, calls=%fused_computation.34 | loop fusion | flops 4718592 | bytes 28311552 | tf_op jit(solution)/shard_map/convert_element_type | solution.py:51
  36.0 1.3 fusion.27
  37.3 0.0 copy-start.8
  37.4 15.6 %fusion.28 = (f32[6,8,255,128]{3,2,1,0:T(8,128)S(1)}, f32[6,8,255,128]{3,2,1,0:T(8,128)}, f32[6,8,255,128]{3,2,1,0:T(8,128)}, f32[6,8,255,128]{3,2,1,0:T(8,128)}) fusion(f32[6,12,256,128]{3,2,1,0:T(8,128)} %get-tuple-element.18, f32[6,12,256,128]{3,2,1,0:T(8,128)} %get-tuple-element.17), kind=kLoop, calls=%fused_computation.46 | loop fusion | bytes 50135040 | tf_op jit(solution)/shard_map/jit(_roll_static)/slice | solution.py:25
  53.0 0.0 copy-done.8
  53.0 0.0 copy-start.10
  53.0 27.2 %fusion.25 = (bf16[6,8,256,128]{3,2,1,0:T(8,128)(2,1)S(1)}, f32[6,8,256,128]{3,2,1,0:T(8,128)}, bf16[6,8,256,128]{3,2,1,0:T(8,128)(2,1)}) fusion(f32[6,12,256,128]{3,2,1,0:T(8,128)} %get-tuple-element.18, f32[6,8,255,128]{3,2,1,0:T(8,128)} %get-tuple-element.24, f32[6,8,1,128]{3,2,1,0:T(1,128)S(1)} %get-tuple-element.22, ...), kind=kLoop, calls=%fused_computation.44 | loop fusion | flops 44040192 | bytes 88088576 | tf_op jit(solution)/shard_map/convert.3
  80.2 0.0 copy-start
  80.2 0.0 copy-done.10
  80.2 0.0 copy-start.2
  80.2 9.8 %fusion.19 = (bf16[6,8,256,128]{3,2,1,0:T(8,128)(2,1)S(1)}, bf16[6,8,256,128]{3,2,1,0:T(8,128)(2,1)}) fusion(f32[6,8,256,128]{3,2,1,0:T(8,128)} %get-tuple-element.6, bf16[6,8,256,128]{3,2,1,0:T(8,128)(2,1)} %param.10, f32[8,256,128]{2,1,0:T(8,128)} %broadcast_multiply_fusion, f32[128]{0:T(128)S(1)} %copy-done.10, bf16[6,8,256,128]{3,2,1,0:T(8,128)(2,1)} %param.11), kind=kLoop, calls=%fused_computation.36 | loop fusion | flops 12582912 | bytes 19923456 | tf_op jit(solution)/shard_map/convert.5
  90.0 0.0 copy-start.6
  90.0 0.0 copy-done
  90.0 1.7 copy-done.6
  91.7 0.0 copy-done.2
  91.7 8.1 %fusion.20 = bf16[8,256,512]{2,1,0:T(8,128)(2,1)} fusion(bf16[6,8,256,128]{3,2,1,0:T(8,128)(2,1)} %get-tuple-element.8, bf16[6,8,256,128]{3,2,1,0:T(8,128)(2,1)S(1)} %get-tuple-element.7, bf16[6,8,256,128]{3,2,1,0:T(8,128)(2,1)S(1)} %copy-done.2, bf16[6,8,256,128]{3,2,1,0:T(8,128)(2,1)S(1)} %get-tuple-element.5), kind=kLoop, calls=%fused_computation.37 | loop fusion | flops 55574528 | bytes 14680064 | tf_op jit(solution)/shard_map/reduce_sum | solution.py:74
  99.8 0.0 copy-start.1
  99.8 0.0 all-reduce.3.cloned.1.call-update
  99.8 0.2 all-reduce.5.cloned.1.call-start
  100.0 86.4 %all-reduce.3.cloned.1.call-done = bf16[8,256,512]{2,1,0:T(8,128)(2,1)} async-done(((bf16[8,256,512]{2,1,0:T(8,128)(2,1)}), bf16[8,256,512]{2,1,0:T(8,128)(2,1)}) %all-reduce.3.cloned.1.call-update) | async-done | bytes 2097168 | tf_op jit(solution)/shard_map/psum | solution.py:76
  186.5 0.0 copy-start.3
  186.5 2.4 convert_multiply_fusion
  188.8 0.0 copy-done.1
  188.8 0.1 copy-done.3
  189.0 47.7 %fusion.21 = f32[512,512]{1,0:T(8,128)} fusion(f32[8,256,512]{2,1,0:T(8,128)S(1)} %convert_multiply_fusion, bf16[6,8,256,128]{3,2,1,0:T(8,128)(2,1)} %get-tuple-element.8, bf16[6,8,256,128]{3,2,1,0:T(8,128)(2,1)} %copy-done.6, bf16[6,8,256,128]{3,2,1,0:T(8,128)(2,1)S(1)} %copy-done.3, bf16[6,8,256,128]{3,2,1,0:T(8,128)(2,1)S(1)} %copy-done.1), kind=kOutput, calls=%fused_computation.40 | convolution fusion | flops 38711328768 | bytes 17825792 | tf_op jit(solution)/shard_map/dot_general | solution.py:29
  236.7 0.0 all-reduce.5.cloned.1.call-update
  236.7 52.7 %all-reduce.5.cloned.1.call-done = f32[512,512]{1,0:T(8,128)} async-done(((f32[512,512]{1,0:T(8,128)}), f32[512,512]{1,0:T(8,128)}) %all-reduce.5.cloned.1.call-update) | async-done | bytes 1048592 | tf_op jit(solution)/shard_map/psum | solution.py:79
  289.4 1.7 multiply_bitcast_fusion
Async XLA Ops:
  6.5 12.3 %copy-start.4 = (bf16[6,8,256,128]{3,2,1,0:T(8,128)(2,1)S(1)}, bf16[6,8,256,128]{3,2,1,0:T(8,128)(2,1)}, u32[]{:S(2)}) copy-start(bf16[6,8,256,128]{3,2,1,0:T(8,128)(2,1)} %param.9) | copy-start | bytes 9437188
  6.5 6.2 %copy-start.7 = (f32[8,256]{1,0:T(8,128)S(1)}, f32[8,256]{1,0:T(8,128)}, u32[]{:S(2)}) copy-start(f32[8,256]{1,0:T(8,128)} %param.13) | copy-start | bytes 24580
  6.5 6.2 %copy-start.9 = (f32[128]{0:T(128)S(1)}, f32[128]{0:T(128)}, u32[]{:S(2)}) copy-start(f32[128]{0:T(128)} %param.14) | copy-start | bytes 1540
  6.5 179.9 %all-reduce.3.cloned.1.call-start = ((), (), s32[]{:S(2)}) async-start(), calls=%async_computation | async-start | bytes 4194304 | tf_op jit(solution)/shard_map/psum | solution.py:76
  6.5 12.3 %copy-start.5 = (bf16[6,8,256,128]{3,2,1,0:T(8,128)(2,1)S(1)}, bf16[6,8,256,128]{3,2,1,0:T(8,128)(2,1)}, u32[]{:S(2)}) copy-start(bf16[6,8,256,128]{3,2,1,0:T(8,128)(2,1)} %param.8) | copy-start | bytes 9437188
  8.8 5.5 %collective-permute-start = (bf16[2,6,2,256,128]{4,3,2,1,0:T(8,128)(2,1)S(1)}, bf16[2,6,2,256,128]{4,3,2,1,0:T(8,128)(2,1)S(1)}, u32[]{:S(2)}, u32[]{:S(2)}) collective-permute-start(bf16[2,6,2,256,128]{4,3,2,1,0:T(8,128)(2,1)S(1)} %get-tuple-element.19), channel_id=1, source_target_pairs={{0,1},{1,2},{2,3},{3,4},{4,5},{5,6},{6,7},{8,9},{9,10},{10,11},{11... | collective-permute-start | bytes 4718600 | tf_op jit(solution)/shard_map/ppermute | solution.py:12
  11.4 7.4 %collective-permute-start.1 = (bf16[2,6,2,256,128]{4,3,2,1,0:T(8,128)(2,1)S(1)}, bf16[2,6,2,256,128]{4,3,2,1,0:T(8,128)(2,1)S(1)}, u32[]{:S(2)}, u32[]{:S(2)}) collective-permute-start(bf16[2,6,2,256,128]{4,3,2,1,0:T(8,128)(2,1)S(1)} %get-tuple-element.20), channel_id=1, source_target_pairs={{1,0},{2,1},{3,2},{4,3},{5,4},{6,5},{7,6},{9,8},{10,9},{11,10},{12... | collective-permute-start | bytes 4718600 | tf_op jit(solution)/shard_map/ppermute | solution.py:15
  37.3 15.7 %copy-start.8 = (f32[8,256]{1,0:T(8,128)S(1)}, f32[8,256]{1,0:T(8,128)}, u32[]{:S(2)}) copy-start(f32[8,256]{1,0:T(8,128)} %param.12) | copy-start | bytes 24580
  53.0 27.2 %copy-start.10 = (f32[128]{0:T(128)S(1)}, f32[128]{0:T(128)}, u32[]{:S(2)}) copy-start(f32[128]{0:T(128)} %param.15) | copy-start | bytes 1540
  80.2 9.8 %copy-start = (bf16[6,8,256,128]{3,2,1,0:T(8,128)(2,1)}, bf16[6,8,256,128]{3,2,1,0:T(8,128)(2,1)S(1)}, u32[]{:S(2)}) copy-start(bf16[6,8,256,128]{3,2,1,0:T(8,128)(2,1)S(1)} %get-tuple-element.5) | copy-start | bytes 9437188
  80.2 11.5 %copy-start.2 = (bf16[6,8,256,128]{3,2,1,0:T(8,128)(2,1)S(1)}, bf16[6,8,256,128]{3,2,1,0:T(8,128)(2,1)}, u32[]{:S(2)}) copy-start(bf16[6,8,256,128]{3,2,1,0:T(8,128)(2,1)} %get-tuple-element.21) | copy-start | bytes 9437188
  90.0 1.7 copy-start.6
  99.8 89.0 %copy-start.1 = (bf16[6,8,256,128]{3,2,1,0:T(8,128)(2,1)S(1)}, bf16[6,8,256,128]{3,2,1,0:T(8,128)(2,1)}, u32[]{:S(2)}) copy-start(bf16[6,8,256,128]{3,2,1,0:T(8,128)(2,1)} %copy-done) | copy-start | bytes 9437188
  99.8 189.6 %all-reduce.5.cloned.1.call-start = ((), (), s32[]{:S(2)}) async-start(), calls=%async_computation.1 | async-start | bytes 2097152 | tf_op jit(solution)/shard_map/psum | solution.py:79
  186.5 2.5 copy-start.3
Sparse Core Ops, SparseCore 0:
  99.9 86.4 all-reduce.2
  236.8 52.5 all-reduce.4
where the time goes:
time: 298 us
  waiting for transfers between devices  144 us (48%)
  other arithmetic  69.9 us (23%)
  matrix products  47.7 us (16%)
  local copies, waits for them, and re-layouts  18.8 us (6%)
  between operations  13.5 us (5%)
  starting transfers between devices  4.11 us (1%)
    psum x1, waiting for transfers between devices, on_device(): lax.psum(local_sum.astype(jnp.bfloat16), 'member').astype(jnp.float32)  86.4 us
    psum x1, waiting for transfers between devices, on_device(): summed = lax.psum(gram_rows(anomaly, anomaly, highest), 'member')  52.7 us
    dot_general x1, matrix products, gram_rows(): lax.dot_general(left, right, (((0,), (0,)), ((), ())), preferred_element_...  47.7 us
    another operation x2, other arithmetic  37 us
    slice x2, local copies, waits for them, and re-layouts, lon_diff(): return (jnp.roll(field, -1, 2) - jnp.roll(field, 1, 2)) / 2.0  17 us
    convert_element_type x1, other arithmetic, on_device(): v_full = padded[1].astype(jnp.float32)  12.8 us
    reduce_sum x1, other arithmetic, on_device(): local_sum = jnp.sum(sample_vector.astype(jnp.float32), axis=0)  8.08 us
  transfers between devices with their start and end apart: 4, of which 4 were waited for; matrix products, arithmetic and copies ran while one was open for 0% of the time, Pallas kernels for 0%

commit v1 on v0

v1 whole, which is shorter than its diff:
```python
import functools

import jax
import jax.numpy as jnp
from jax import lax
from jax.experimental import pallas as pl
from jax.experimental.pallas import tpu as pltpu
from jax.sharding import PartitionSpec as P

CHUNK = 16


def moments_kernel(rows, halo, *refs):
    u_hbm, v_hbm, h_hbm, q_hbm, f_hbm, c_hbm = refs[:6]
    refs = refs[6:]
    if halo:
        low_hbm, high_hbm, start_ref = refs[:3]
        refs = refs[3:]
    shift_ref, slope_ref, mean_ref, moment_ref = refs[:4]
    u, v, h, q, f, c, dlon, anom, wind_sem, rest_sem, halo_sem = refs[4:]
    members, extended, lons, levels = u.shape
    height = extended - 4
    need = sorted({r + d for r in rows for d in range(-2, 3)})
    own = [r for r in need if 0 <= r < height]
    wind_copies, rest_copies, halo_copies = {}, {}, []
    for r in own:
        wind_copies[r] = [
            pltpu.make_async_copy(src.at[:, r], dst.at[:, r + 2], wind_sem.at[r, k])
            for k, (src, dst) in enumerate(((u_hbm, u), (v_hbm, v)))
        ]
    for k, r in enumerate(rows):
        rest_copies[k] = [
            pltpu.make_async_copy(h_hbm.at[:, r], h.at[k], rest_sem.at[k, 0]),
            pltpu.make_async_copy(q_hbm.at[:, r], q.at[k], rest_sem.at[k, 1]),
            pltpu.make_async_copy(f_hbm.at[r], f.at[k], rest_sem.at[k, 2]),
            pltpu.make_async_copy(c_hbm.at[r], c.at[k], rest_sem.at[k, 3]),
        ]
    if halo:
        for k, dst in enumerate((u, v)):
            halo_copies.append(
                pltpu.make_async_copy(low_hbm.at[k], dst.at[:, pl.ds(0, 2)], halo_sem.at[0, k])
            )
            halo_copies.append(
                pltpu.make_async_copy(
                    high_hbm.at[k], dst.at[:, pl.ds(extended - 2, 2)], halo_sem.at[1, k]
                )
            )
    for copy in halo_copies:
        copy.start()
    for r in own:
        for copy in wind_copies[r]:
            copy.start()
        if r in rows:
            for copy in rest_copies[rows.index(r)]:
                copy.start()
    if halo:
        moment_ref[...] = start_ref[...]
    else:
        moment_ref[...] = jnp.zeros_like(moment_ref)
    for copy in halo_copies:
        copy.wait()
    waited = set()
    for k, r in enumerate(rows):
        for d in range(-2, 3):
            if r + d in wind_copies and r + d not in waited:
                waited.add(r + d)
                for copy in wind_copies[r + d]:
                    copy.wait()
        for copy in rest_copies[k]:
            copy.wait()
        e = r + 2
        for m in range(members):
            both = jnp.concatenate([v[m, e], u[m, e]], axis=1)
            dlon[m] = jnp.dot(shift_ref[...], both, preferred_element_type=jnp.float32)

        def chunk(j, carry):
            at = pl.ds(pl.multiple_of(j * CHUNK, CHUNK), CHUNK)
            factor = f[k, at, :]
            curl_factor = c[k, at, :]
            slope = slope_ref[...]
            held, total = [], None
            for m in range(members):
                def wind(ref, d):
                    return ref[m, e + d, at, :].astype(jnp.float32)

                def lat(ref):
                    return 8.0 * (wind(ref, 1) - wind(ref, -1)) - (wind(ref, 2) - wind(ref, -2))

                curl = factor * (dlon[m, at, :levels] - lat(u))
                spread = factor * (dlon[m, at, levels:] + lat(v))
                heat = h[k, m, at, :].astype(jnp.float32) - curl_factor * curl
                moist = q[k, m, at, :].astype(jnp.float32) - slope * heat
                state = (curl, spread, heat, moist)
                held.append(state)
                total = state if total is None else tuple(a + b for a, b in zip(total, state))
            mean = tuple(a * (1.0 / members) for a in total)
            for n in range(4):
                lanes = slice(n * levels, (n + 1) * levels)
                mean_ref[k, at, lanes] = mean[n].astype(jnp.bfloat16)
                for m in range(members):
                    anom[m, at, lanes] = (held[m][n] - mean[n]).astype(jnp.bfloat16)
            return carry

        lax.fori_loop(0, lons // CHUNK, chunk, 0)
        for m in range(members):
            a = anom[m]
            moment_ref[...] += lax.dot_general(
                a, a, (((0,), (0,)), ((), ())), preferred_element_type=jnp.float32
            )


def moments(rows, fields, factors, shift, slope, halos=None, start=None):
    members, height, lons, levels = fields[0].shape
    count, width = len(rows), 4 * levels
    halo = halos is not None
    hbm = pl.BlockSpec(memory_space=pl.ANY)
    vmem = pl.BlockSpec(memory_space=pltpu.VMEM)
    operands = list(fields) + list(factors)
    specs = [hbm] * 6
    if halo:
        operands += list(halos) + [start]
        specs += [hbm, hbm, vmem]
    operands += [shift, slope]
    specs += [vmem, vmem]
    bf16, f32 = jnp.bfloat16, jnp.float32
    return pl.pallas_call(
        functools.partial(moments_kernel, rows, halo),
        out_shape=(
            jax.ShapeDtypeStruct((count, lons, width), bf16),
            jax.ShapeDtypeStruct((width, width), f32),
        ),
        in_specs=specs,
        out_specs=(vmem, vmem),
        scratch_shapes=[
            pltpu.VMEM((members, height + 4, lons, levels), bf16),
            pltpu.VMEM((members, height + 4, lons, levels), bf16),
            pltpu.VMEM((count, members, lons, levels), bf16),
            pltpu.VMEM((count, members, lons, levels), bf16),
            pltpu.VMEM((count, lons, levels), f32),
            pltpu.VMEM((count, lons, levels), f32),
            pltpu.VMEM((members, lons, 2 * levels), f32),
            pltpu.VMEM((members, lons, width), bf16),
            pltpu.SemaphoreType.DMA((height, 2)),
            pltpu.SemaphoreType.DMA((count, 4)),
            pltpu.SemaphoreType.DMA((2, 2)),
        ],
        compiler_params=pltpu.CompilerParams(vmem_limit_bytes=40 * 2**20),
        cost_estimate=pl.CostEstimate(
            flops=2 * count * members * lons * width * width * 2,
            bytes_accessed=12 * 2**20,
            transcendentals=0,
        ),
        name="halo_moments" if halo else "inner_moments",
    )(*operands)


def edge_rows(winds, axis):
    count = lax.axis_size(axis)
    forward = [(i, i + 1) for i in range(count - 1)]
    backward = [(b, a) for a, b in forward]
    low = jnp.stack([w[:, -2:] for w in winds])
    high = jnp.stack([w[:, :2] for w in winds])
    return lax.ppermute(low, axis, forward), lax.ppermute(high, axis, backward)


def shares(whole, axis):
    count = lax.axis_size(axis)
    me = lax.axis_index(axis)
    size = whole.shape[0] // count
    got = [lax.dynamic_slice_in_dim(whole, me * size, size, 0)]
    for k in range(1, count):
        target = me ^ k
        block = lax.dynamic_slice_in_dim(whole, target * size, size, 0)
        got.append(lax.ppermute(block, axis, [(i, i ^ k) for i in range(count)]))
    return got


def between(means, axis):
    got = jnp.stack(shares(means.reshape(-1, means.shape[-1]), axis)).astype(jnp.float32)
    away = (got - jnp.mean(got, axis=0, keepdims=True)).astype(jnp.bfloat16)
    return away.reshape(-1, away.shape[-1])


def on_device(u, v, h, q, projection_scale, balance_multiplier, heat_slope, moist_slope):
    members, height, lons, levels = u.shape
    groups = lax.axis_size("member")
    scale = 1.0 / ((members * groups - 1) * height * lons)
    shape = (height, lons, levels)
    factor = jnp.broadcast_to((projection_scale / 12.0)[:, :, None], shape)
    curl_factor = balance_multiplier[:, :, None] * heat_slope
    eye = jnp.eye(lons, dtype=jnp.bfloat16)
    shift = 6.0 * (jnp.roll(eye, 1, 1) - jnp.roll(eye, -1, 1))
    slope = moist_slope[None]
    fields, factors = (u, v, h, q), (factor, curl_factor)
    halos = edge_rows((u, v), "space")
    inner = tuple(range(2, height - 2))
    outer = (0, 1, height - 2, height - 1)
    inner_mean, start = moments(inner, fields, factors, shift, slope)
    inner_away = between(inner_mean, "member")
    outer_mean, moment = moments(outer, fields, factors, shift, slope, halos, start)
    outer_away = between(outer_mean, "member")
    away = jnp.concatenate([inner_away, outer_away])
    moment += members * lax.dot_general(
        away, away, (((0,), (0,)), ((), ())), preferred_element_type=jnp.float32
    )
    return (sum(shares(moment, "member")) * scale)[None]


def solution(mesh):
    placed = (
        P("member", "space", None, None),
        P("member", "space", None, None),
        P("member", "space", None, None),
        P("member", "space", None, None),
        P("space", None),
        P("space", None),
        P(),
        P(),
    )
    return jax.shard_map(
        on_device, mesh=mesh, in_specs=placed, out_specs=P("space", "member", None), check_vma=False
    )
```

time: 298 us -> 96.1 us (0.32)
  waiting for transfers between devices: 144 us -> 34.3 us
  other arithmetic: 69.9 us -> 7.3 us
  matrix products: 47.7 us -> 1.28 us
  Pallas kernels: 0 us -> 25.4 us
  between operations: 13.5 us -> 0.22 us
  starting transfers between devices: 4.11 us -> 16 us
  local copies, waits for them, and re-layouts: 18.8 us -> 11.2 us
    psum x2 -> x0, waiting for transfers between devices: 139 us -> none  [the longest x1 86.4 us: on_device(): lax.psum(local_sum.astype(jnp.bfloat16), 'member').astype(jnp.float32)]
    dot_general x1, matrix products: 47.7 us -> 1.28 us  [on_device(): lax.dot_general(away, away, (((0,), (0,)), ((), ())), preferred_element_t...]
    another operation x2, other arithmetic: 37 us -> 2.6 us  [the longest x1 1.33 us: edge_rows(): high = jnp.stack([w[:, :2] for w in winds])]
    ppermute x2 -> x11, waiting for transfers between devices: 4.73 us -> 34.3 us  [the longest x9 34.3 us: shares(): got.append(lax.ppermute(block, axis, [(i, i ^ k) for i in range(count)]))]
    pallas_call x0 -> x2, Pallas kernels: none -> 25.4 us  [moments(): pl.pallas_call(functools.partial(moments_kernel, rows, halo), out_shape=(...]
    slice x2, local copies, waits for them, and re-layouts: 17 us -> 0.19 us  [on_device(): shift = 6.0 * (jnp.roll(eye, 1, 1) - jnp.roll(eye, -1, 1))]
    ppermute x2 -> x11, starting transfers between devices: 3.88 us -> 16 us  [the longest x9 11 us: shares(): got.append(lax.ppermute(block, axis, [(i, i ^ k) for i in range(count)]))]
    convert_element_type x1 -> x3, other arithmetic: 12.8 us -> 1.68 us  [the longest x2 1.66 us: between(): away = (got - jnp.mean(got, axis=0, keepdims=True)).astype(jnp.bfloat16)]
  transfers between devices with their start and end apart: 4 -> 11, of which waited for: 4 -> 9; matrix products, arithmetic and copies ran while one was open for 0% -> 6% of each run, Pallas kernels for 0% -> 13%
where the time goes in v1:
time: 96.1 us; the launch traced here: 95.7 us
  waiting for transfers between devices  34.3 us (36%)
  Pallas kernels  25.4 us (26%)
  starting transfers between devices  16 us (17%)
  local copies, waits for them, and re-layouts  11.2 us (12%)
  other arithmetic  7.3 us (8%)
  matrix products  1.28 us (1%)
    ppermute x9, waiting for transfers between devices, shares(): got.append(lax.ppermute(block, axis, [(i, i ^ k) for i in range(count)]))  34.3 us
    pallas_call x2, Pallas kernels, moments(): pl.pallas_call(functools.partial(moments_kernel, rows, halo), out_shape=(...  25.4 us
    ppermute x9, starting transfers between devices, shares(): got.append(lax.ppermute(block, axis, [(i, i ^ k) for i in range(count)]))  11 us
    unnamed x16, local copies, waits for them, and re-layouts  7.56 us
    ppermute x1, starting transfers between devices, edge_rows(): lax.ppermute(low, axis, forward)  3.65 us
    another operation x1, local copies, waits for them, and re-layouts, edge_rows(): high = jnp.stack([w[:, :2] for w in winds])  2.05 us
  transfers between devices with their start and end apart: 11, of which 9 were waited for; matrix products, arithmetic and copies ran while one was open for 6% of the time, Pallas kernels for 13%

profile of v1, /device:TPU:0, one launch (start us, length us, event | category | flops | bytes accessed | tf_op | source)
XLA Modules:
  0.0 95.7 jit_solution(3608617787064720394)
XLA Ops:
  0.0 2.0 %slice_bitcast_fusion = (bf16[1,6,2,256,128]{4,3,2,1,0:T(8,128)(2,1)S(1)}, bf16[1,6,2,256,128]{4,3,2,1,0:T(8,128)(2,1)S(1)}, bf16[1,6,2,256,128]{4,3,2,1,0:T(8,128)(2,1)S(1)}, bf16[1,6,2,256,128]{4,3,2,1,0:T(8,128)(2,1)S(1)}) fusion(bf16[6,8,256,128]{3,2,1,0:T(8,128)(2,1)} %refs_1_.3, bf16[6,8,256,128]{3,2,1,0:T(8,128)(2,1)} %refs_0_.3), kind=kLoop, calls=%fused_computation.15 | loop fusion | bytes 6291456 | tf_op jit(solution)/shard_map/stack | solution.py:162
  2.1 1.3 %pad_maximum_fusion = bf16[2,6,2,256,128]{4,3,2,1,0:T(8,128)(2,1)} fusion(bf16[1,6,2,256,128]{4,3,2,1,0:T(8,128)(2,1)S(1)} %get-tuple-element.16, bf16[1,6,2,256,128]{4,3,2,1,0:T(8,128)(2,1)S(1)} %get-tuple-element.32), kind=kLoop, calls=%fused_computation.10 | loop fusion | flops 786432 | bytes 3145728 | tf_op jit(solution)/shard_map/stack | solution.py:161
  3.3 0.0 copy-start.5
  3.3 0.0 copy-start.7
  3.3 3.7 %collective-permute-start = (bf16[2,6,2,256,128]{4,3,2,1,0:T(8,128)(2,1)}, bf16[2,6,2,256,128]{4,3,2,1,0:T(8,128)(2,1)}, u32[]{:S(2)}, u32[]{:S(2)}) collective-permute-start(bf16[2,6,2,256,128]{4,3,2,1,0:T(8,128)(2,1)} %pad_maximum_fusion), channel_id=1, source_target_pairs={{0,1},{1,2},{2,3},{3,4},{4,5},{5,6},{6,7},{8,9},{9,10},{10,11},{11... | collective-permute-start | bytes 4718600 | tf_op jit(solution)/shard_map/ppermute | solution.py:163
  7.0 0.0 copy-start.6
  7.0 1.3 %pad_maximum_fusion.1 = bf16[2,6,2,256,128]{4,3,2,1,0:T(8,128)(2,1)} fusion(bf16[1,6,2,256,128]{4,3,2,1,0:T(8,128)(2,1)S(1)} %get-tuple-element.15, bf16[1,6,2,256,128]{4,3,2,1,0:T(8,128)(2,1)S(1)} %get-tuple-element.33), kind=kLoop, calls=%fused_computation.11 | loop fusion | flops 786432 | bytes 3145728 | tf_op jit(solution)/shard_map/stack | solution.py:162
  8.3 0.0 copy-start.4
  8.3 1.4 %collective-permute-start.1 = (bf16[2,6,2,256,128]{4,3,2,1,0:T(8,128)(2,1)}, bf16[2,6,2,256,128]{4,3,2,1,0:T(8,128)(2,1)}, u32[]{:S(2)}, u32[]{:S(2)}) collective-permute-start(bf16[2,6,2,256,128]{4,3,2,1,0:T(8,128)(2,1)} %pad_maximum_fusion.1), channel_id=1, source_target_pairs={{1,0},{2,1},{3,2},{4,3},{5,4},{6,5},{7,6},{9,8},{10,9},{11,10},{12... | collective-permute-start | bytes 4718600 | tf_op jit(solution)/shard_map/ppermute | solution.py:163
  9.8 0.1 fusion.9
  9.9 0.1 fusion.10
  10.0 0.0 copy-done.5
  10.0 0.0 copy-done.7
  10.0 0.3 broadcast_multiply_fusion.refs_5_
  10.3 0.1 fusion.7.refs_6_.refs_9_
  10.5 0.0 copy-done.6
  10.5 0.3 broadcast_in_dim.6.refs_4_
  10.8 0.0 copy-done.4
  10.8 0.0 copy-start
  10.9 1.9 %copy-done = bf16[6,8,256,128]{3,2,1,0:T(8,128)(2,1)S(1)} copy-done((bf16[6,8,256,128]{3,2,1,0:T(8,128)(2,1)S(1)}, bf16[6,8,256,128]{3,2,1,0:T(8,128)(2,1)}, u32[]{:S(2)}) %copy-start) | copy-done | bytes 3145752
  12.7 0.0 copy-start.2
  12.7 1.9 %copy-done.2 = bf16[6,8,256,128]{3,2,1,0:T(8,128)(2,1)S(1)} copy-done((bf16[6,8,256,128]{3,2,1,0:T(8,128)(2,1)S(1)}, bf16[6,8,256,128]{3,2,1,0:T(8,128)(2,1)}, u32[]{:S(2)}) %copy-start.2) | copy-done | bytes 3145752
  14.6 0.0 copy-start.3
  14.6 1.9 %copy-done.3 = bf16[6,8,256,128]{3,2,1,0:T(8,128)(2,1)S(1)} copy-done((bf16[6,8,256,128]{3,2,1,0:T(8,128)(2,1)S(1)}, bf16[6,8,256,128]{3,2,1,0:T(8,128)(2,1)}, u32[]{:S(2)}) %copy-start.3) | copy-done | bytes 3145752
  16.5 12.4 %inner_moments.1 = (bf16[4,256,512]{2,1,0:T(8,128)(2,1)S(1)}, f32[512,512]{1,0:T(8,128)S(1)}) custom-call(bf16[6,8,256,128]{3,2,1,0:T(8,128)(2,1)S(1)} %copy-done, bf16[6,8,256,128]{3,2,1,0:T(8,128)(2,1)S(1)} %copy-done.2, bf16[6,8,256,128]{3,2,1,0:T(8,128)(2,1)S(1)} %copy-done.3, bf16[6,8,256,128]{3,2,1,0:T(8,128)(2,1)} %refs_3_.3, ...), custom_call_target="tpu_custom_call" | custom-call | flops 6442450944 | bytes 12582912 | tf_op jit(solution)/shard_map/inner_moments/pallas_call | solution.py:126
  28.9 0.9 dynamic-slice_bitcast_fusion.1
  29.8 3.3 %collective-permute-start.4 = (bf16[256,512]{1,0:T(8,128)(2,1)}, bf16[256,512]{1,0:T(8,128)(2,1)}, u32[]{:S(2)}, u32[]{:S(2)}) collective-permute-start(bf16[256,512]{1,0:T(8,128)(2,1)} %get-tuple-element.21), channel_id=1, source_target_pairs={{0,24},{8,16},{16,8},{24,0},{1,25},{9,17},{17,9},{25,1},{2,26},{10... | collective-permute-start | bytes 786440 | tf_op jit(solution)/shard_map/ppermute | solution.py:174
  33.1 0.5 collective-permute-start.3
  33.6 0.1 collective-permute-start.2
  33.7 6.2 %collective-permute-done.4 = bf16[256,512]{1,0:T(8,128)(2,1)} collective-permute-done((bf16[256,512]{1,0:T(8,128)(2,1)}, bf16[256,512]{1,0:T(8,128)(2,1)}, u32[]{:S(2)}, u32[]{:S(2)}) %collective-permute-start.4) | collective-permute-done | bytes 262176 | tf_op jit(solution)/shard_map/ppermute | solution.py:174
  39.9 6.3 %collective-permute-done.3 = bf16[256,512]{1,0:T(8,128)(2,1)} collective-permute-done((bf16[256,512]{1,0:T(8,128)(2,1)}, bf16[256,512]{1,0:T(8,128)(2,1)}, u32[]{:S(2)}, u32[]{:S(2)}) %collective-permute-start.3) | collective-permute-done | bytes 262176 | tf_op jit(solution)/shard_map/ppermute | solution.py:174
  46.2 0.3 collective-permute-done.2
  46.5 1.3 %convert_reduce_fusion.1 = f32[256,512]{1,0:T(8,128)S(1)} fusion(bf16[1,256,512]{2,1,0:T(8,128)(2,1)} %bitcast.9, bf16[1,256,512]{2,1,0:T(8,128)(2,1)} %bitcast.8, bf16[1,256,512]{2,1,0:T(8,128)(2,1)} %bitcast.7, bf16[1,256,512]{2,1,0:T(8,128)(2,1)S(1)} %get-tuple-element.20), kind=kLoop, calls=%fused_computation.3 | loop fusion | flops 2490368 | bytes 1572864 | tf_op jit(solution)/shard_map/reduce_sum | solution.py:180
  47.9 0.0 collective-permute-done.refs_6_
  47.9 0.0 collective-permute-done.1.refs_7_
  47.9 0.0 copy-start.1
  47.9 1.9 %copy-done.1 = bf16[6,8,256,128]{3,2,1,0:T(8,128)(2,1)S(1)} copy-done((bf16[6,8,256,128]{3,2,1,0:T(8,128)(2,1)S(1)}, bf16[6,8,256,128]{3,2,1,0:T(8,128)(2,1)}, u32[]{:S(2)}) %copy-start.1) | copy-done | bytes 3145752
  49.8 13.0 %halo_moments.1 = (bf16[4,256,512]{2,1,0:T(8,128)(2,1)S(1)}, f32[512,512]{1,0:T(8,128)S(1)}) custom-call(bf16[6,8,256,128]{3,2,1,0:T(8,128)(2,1)S(1)} %copy-done.1, bf16[6,8,256,128]{3,2,1,0:T(8,128)(2,1)} %refs_1_.3, bf16[6,8,256,128]{3,2,1,0:T(8,128)(2,1)} %refs_2_.3, bf16[6,8,256,128]{3,2,1,0:T(8,128)(2,1)} %refs_3_.3, ...), custom_call_target="tpu_custom_call" | custom-call | flops 6442450944 | bytes 12582912 | tf_op jit(solution)/shard_map/halo_moments/pallas_call | solution.py:126
  62.8 0.1 dynamic-slice_bitcast_fusion
  62.9 1.5 %collective-permute-start.7 = (bf16[256,512]{1,0:T(8,128)(2,1)S(1)}, bf16[256,512]{1,0:T(8,128)(2,1)S(1)}, u32[]{:S(2)}, u32[]{:S(2)}) collective-permute-start(bf16[256,512]{1,0:T(8,128)(2,1)S(1)} %get-tuple-element.25), channel_id=1, source_target_pairs={{0,24},{8,16},{16,8},{24,0},{1,25},{9,17},{17,9},{25,1},{2,26},{10... | collective-permute-start | bytes 786440 | tf_op jit(solution)/shard_map/ppermute | solution.py:174
  64.4 1.7 %collective-permute-start.6 = (bf16[256,512]{1,0:T(8,128)(2,1)S(1)}, bf16[256,512]{1,0:T(8,128)(2,1)S(1)}, u32[]{:S(2)}, u32[]{:S(2)}) collective-permute-start(bf16[256,512]{1,0:T(8,128)(2,1)S(1)} %get-tuple-element.26), channel_id=1, source_target_pairs={{0,16},{8,24},{16,0},{24,8},{1,17},{9,25},{17,1},{25,9},{2,18},{10... | collective-permute-start | bytes 786440 | tf_op jit(solution)/shard_map/ppermute | solution.py:174
  66.1 0.4 collective-permute-start.5
  66.4 1.4 %fusion = bf16[4,256,512]{2,1,0:T(8,128)(2,1)S(1)} fusion(f32[256,512]{1,0:T(8,128)S(1)} %broadcast_multiply_fusion.2, bf16[1,256,512]{2,1,0:T(8,128)(2,1)} %bitcast.9, bf16[1,256,512]{2,1,0:T(8,128)(2,1)} %bitcast.8, bf16[1,256,512]{2,1,0:T(8,128)(2,1)} %bitcast.7, bf16[1,256,512]{2,1,0:T(8,128)(2,1)S(1)} %get-tuple-element.20), kind=kLoop, calls=%fused_computation.4 | loop fusion | flops 3145728 | bytes 2621440 | tf_op jit(solution)/shard_map/convert_element_type | solution.py:180
  67.8 5.2 %collective-permute-done.7 = bf16[256,512]{1,0:T(8,128)(2,1)S(1)} collective-permute-done((bf16[256,512]{1,0:T(8,128)(2,1)S(1)}, bf16[256,512]{1,0:T(8,128)(2,1)S(1)}, u32[]{:S(2)}, u32[]{:S(2)}) %collective-permute-start.7) | collective-permute-done | bytes 262176 | tf_op jit(solution)/shard_map/ppermute | solution.py:174
  73.0 4.7 %collective-permute-done.6 = bf16[256,512]{1,0:T(8,128)(2,1)S(1)} collective-permute-done((bf16[256,512]{1,0:T(8,128)(2,1)S(1)}, bf16[256,512]{1,0:T(8,128)(2,1)S(1)}, u32[]{:S(2)}, u32[]{:S(2)}) %collective-permute-start.6) | collective-permute-done | bytes 262176 | tf_op jit(solution)/shard_map/ppermute | solution.py:174
  77.8 0.3 collective-permute-done.5
  78.1 0.2 convert_reduce_fusion
  78.3 0.3 fusion.1
  78.6 1.3 %fusion.2 = f32[512,512]{1,0:T(8,128)S(1)} fusion(bf16[1024,512]{1,0:T(8,128)(2,1)S(1)} %bitcast.30, bf16[1024,512]{1,0:T(8,128)(2,1)S(1)} %bitcast.29), kind=kOutput, calls=%fused_computation.6 | convolution fusion | flops 1077936128 | bytes 3145728 | tf_op jit(solution)/shard_map/dot_general | solution.py:203
  79.8 0.2 multiply_add_fusion
  80.1 0.1 constant_dynamic-slice_fusion.2
  80.1 1.5 %collective-permute-start.10 = (f32[128,512]{1,0:T(8,128)S(1)}, f32[128,512]{1,0:T(8,128)S(1)}, u32[]{:S(2)}, u32[]{:S(2)}) collective-permute-start(f32[128,512]{1,0:T(8,128)S(1)} %get-tuple-element.18), channel_id=1, source_target_pairs={{0,24},{8,16},{16,8},{24,0},{1,25},{9,17},{17,9},{25,1},{2,26},{10... | collective-permute-start | bytes 786440 | tf_op jit(solution)/shard_map/ppermute | solution.py:174
  81.6 1.4 %collective-permute-start.9 = (f32[128,512]{1,0:T(8,128)S(1)}, f32[128,512]{1,0:T(8,128)S(1)}, u32[]{:S(2)}, u32[]{:S(2)}) collective-permute-start(f32[128,512]{1,0:T(8,128)S(1)} %get-tuple-element.19), channel_id=1, source_target_pairs={{0,16},{8,24},{16,0},{24,8},{1,17},{9,25},{17,1},{25,9},{2,18},{10... | collective-permute-start | bytes 786440 | tf_op jit(solution)/shard_map/ppermute | solution.py:174
  83.1 0.6 collective-permute-start.8
  83.7 6.7 %collective-permute-done.10 = f32[128,512]{1,0:T(8,128)S(1)} collective-permute-done((f32[128,512]{1,0:T(8,128)S(1)}, f32[128,512]{1,0:T(8,128)S(1)}, u32[]{:S(2)}, u32[]{:S(2)}) %collective-permute-start.10) | collective-permute-done | bytes 262176 | tf_op jit(solution)/shard_map/ppermute | solution.py:174
  90.4 4.3 %collective-permute-done.9 = f32[128,512]{1,0:T(8,128)S(1)} collective-permute-done((f32[128,512]{1,0:T(8,128)S(1)}, f32[128,512]{1,0:T(8,128)S(1)}, u32[]{:S(2)}, u32[]{:S(2)}) %collective-permute-start.9) | collective-permute-done | bytes 262176 | tf_op jit(solution)/shard_map/ppermute | solution.py:174
  94.7 0.3 collective-permute-done.8
  95.0 0.8 multiply_bitcast_fusion
  (4 shorter events, 0.1 us)
Async XLA Ops:
  3.3 6.6 %copy-start.5 = (f32[8,256]{1,0:T(8,128)S(1)}, f32[8,256]{1,0:T(8,128)}, u32[]{:S(2)}) copy-start(f32[8,256]{1,0:T(8,128)} %param.13) | copy-start | bytes 24580
  3.3 6.7 %copy-start.7 = (f32[128]{0:T(128)S(1)}, f32[128]{0:T(128)}, u32[]{:S(2)}) copy-start(f32[128]{0:T(128)} %param.14) | copy-start | bytes 1540
  3.3 44.5 %collective-permute-start = (bf16[2,6,2,256,128]{4,3,2,1,0:T(8,128)(2,1)}, bf16[2,6,2,256,128]{4,3,2,1,0:T(8,128)(2,1)}, u32[]{:S(2)}, u32[]{:S(2)}) collective-permute-start(bf16[2,6,2,256,128]{4,3,2,1,0:T(8,128)(2,1)} %pad_maximum_fusion), channel_id=1, source_target_pairs={{0,1},{1,2},{2,3},{3,4},{4,5},{5,6},{6,7},{8,9},{9,10},{10,11},{11... | collective-permute-start | bytes 4718600 | tf_op jit(solution)/shard_map/ppermute | solution.py:163
  7.0 3.5 %copy-start.6 = (f32[8,256]{1,0:T(8,128)S(1)}, f32[8,256]{1,0:T(8,128)}, u32[]{:S(2)}) copy-start(f32[8,256]{1,0:T(8,128)} %param.12) | copy-start | bytes 24580
  8.3 2.5 %copy-start.4 = (f32[128]{0:T(128)S(1)}, f32[128]{0:T(128)}, u32[]{:S(2)}) copy-start(f32[128]{0:T(128)} %param.15) | copy-start | bytes 1540
  8.3 39.6 %collective-permute-start.1 = (bf16[2,6,2,256,128]{4,3,2,1,0:T(8,128)(2,1)}, bf16[2,6,2,256,128]{4,3,2,1,0:T(8,128)(2,1)}, u32[]{:S(2)}, u32[]{:S(2)}) collective-permute-start(bf16[2,6,2,256,128]{4,3,2,1,0:T(8,128)(2,1)} %pad_maximum_fusion.1), channel_id=1, source_target_pairs={{1,0},{2,1},{3,2},{4,3},{5,4},{6,5},{7,6},{9,8},{10,9},{11,10},{12... | collective-permute-start | bytes 4718600 | tf_op jit(solution)/shard_map/ppermute | solution.py:163
  10.8 1.9 %copy-start = (bf16[6,8,256,128]{3,2,1,0:T(8,128)(2,1)S(1)}, bf16[6,8,256,128]{3,2,1,0:T(8,128)(2,1)}, u32[]{:S(2)}) copy-start(bf16[6,8,256,128]{3,2,1,0:T(8,128)(2,1)} %refs_0_.3) | copy-start | bytes 9437188
  12.7 1.9 %copy-start.2 = (bf16[6,8,256,128]{3,2,1,0:T(8,128)(2,1)S(1)}, bf16[6,8,256,128]{3,2,1,0:T(8,128)(2,1)}, u32[]{:S(2)}) copy-start(bf16[6,8,256,128]{3,2,1,0:T(8,128)(2,1)} %refs_1_.3) | copy-start | bytes 9437188
  14.6 1.9 %copy-start.3 = (bf16[6,8,256,128]{3,2,1,0:T(8,128)(2,1)S(1)}, bf16[6,8,256,128]{3,2,1,0:T(8,128)(2,1)}, u32[]{:S(2)}) copy-start(bf16[6,8,256,128]{3,2,1,0:T(8,128)(2,1)} %refs_2_.3) | copy-start | bytes 9437188
  29.8 10.1 %collective-permute-start.4 = (bf16[256,512]{1,0:T(8,128)(2,1)}, bf16[256,512]{1,0:T(8,128)(2,1)}, u32[]{:S(2)}, u32[]{:S(2)}) collective-permute-start(bf16[256,512]{1,0:T(8,128)(2,1)} %get-tuple-element.21), channel_id=1, source_target_pairs={{0,24},{8,16},{16,8},{24,0},{1,25},{9,17},{17,9},{25,1},{2,26},{10... | collective-permute-start | bytes 786440 | tf_op jit(solution)/shard_map/ppermute | solution.py:174
  33.1 13.1 %collective-permute-start.3 = (bf16[256,512]{1,0:T(8,128)(2,1)}, bf16[256,512]{1,0:T(8,128)(2,1)}, u32[]{:S(2)}, u32[]{:S(2)}) collective-permute-start(bf16[256,512]{1,0:T(8,128)(2,1)} %get-tuple-element.22), channel_id=1, source_target_pairs={{0,16},{8,24},{16,0},{24,8},{1,17},{9,25},{17,1},{25,9},{2,18},{10... | collective-permute-start | bytes 786440 | tf_op jit(solution)/shard_map/ppermute | solution.py:174
  33.6 12.9 %collective-permute-start.2 = (bf16[256,512]{1,0:T(8,128)(2,1)}, bf16[256,512]{1,0:T(8,128)(2,1)}, u32[]{:S(2)}, u32[]{:S(2)}) collective-permute-start(bf16[256,512]{1,0:T(8,128)(2,1)} %get-tuple-element.23), channel_id=1, source_target_pairs={{0,8},{8,0},{16,24},{24,16},{1,9},{9,1},{17,25},{25,17},{2,10},{10... | collective-permute-start | bytes 786440 | tf_op jit(solution)/shard_map/ppermute | solution.py:174
  47.9 1.9 %copy-start.1 = (bf16[6,8,256,128]{3,2,1,0:T(8,128)(2,1)S(1)}, bf16[6,8,256,128]{3,2,1,0:T(8,128)(2,1)}, u32[]{:S(2)}) copy-start(bf16[6,8,256,128]{3,2,1,0:T(8,128)(2,1)} %refs_0_.3) | copy-start | bytes 9437188
  62.9 10.2 %collective-permute-start.7 = (bf16[256,512]{1,0:T(8,128)(2,1)S(1)}, bf16[256,512]{1,0:T(8,128)(2,1)S(1)}, u32[]{:S(2)}, u32[]{:S(2)}) collective-permute-start(bf16[256,512]{1,0:T(8,128)(2,1)S(1)} %get-tuple-element.25), channel_id=1, source_target_pairs={{0,24},{8,16},{16,8},{24,0},{1,25},{9,17},{17,9},{25,1},{2,26},{10... | collective-permute-start | bytes 786440 | tf_op jit(solution)/shard_map/ppermute | solution.py:174
  64.4 13.4 %collective-permute-start.6 = (bf16[256,512]{1,0:T(8,128)(2,1)S(1)}, bf16[256,512]{1,0:T(8,128)(2,1)S(1)}, u32[]{:S(2)}, u32[]{:S(2)}) collective-permute-start(bf16[256,512]{1,0:T(8,128)(2,1)S(1)} %get-tuple-element.26), channel_id=1, source_target_pairs={{0,16},{8,24},{16,0},{24,8},{1,17},{9,25},{17,1},{25,9},{2,18},{10... | collective-permute-start | bytes 786440 | tf_op jit(solution)/shard_map/ppermute | solution.py:174
  66.1 12.0 %collective-permute-start.5 = (bf16[256,512]{1,0:T(8,128)(2,1)S(1)}, bf16[256,512]{1,0:T(8,128)(2,1)S(1)}, u32[]{:S(2)}, u32[]{:S(2)}) collective-permute-start(bf16[256,512]{1,0:T(8,128)(2,1)S(1)} %get-tuple-element.27), channel_id=1, source_target_pairs={{0,8},{8,0},{16,24},{24,16},{1,9},{9,1},{17,25},{25,17},{2,10},{10... | collective-permute-start | bytes 786440 | tf_op jit(solution)/shard_map/ppermute | solution.py:174
  80.1 10.2 %collective-permute-start.10 = (f32[128,512]{1,0:T(8,128)S(1)}, f32[128,512]{1,0:T(8,128)S(1)}, u32[]{:S(2)}, u32[]{:S(2)}) collective-permute-start(f32[128,512]{1,0:T(8,128)S(1)} %get-tuple-element.18), channel_id=1, source_target_pairs={{0,24},{8,16},{16,8},{24,0},{1,25},{9,17},{17,9},{25,1},{2,26},{10... | collective-permute-start | bytes 786440 | tf_op jit(solution)/shard_map/ppermute | solution.py:174
  81.6 13.0 %collective-permute-start.9 = (f32[128,512]{1,0:T(8,128)S(1)}, f32[128,512]{1,0:T(8,128)S(1)}, u32[]{:S(2)}, u32[]{:S(2)}) collective-permute-start(f32[128,512]{1,0:T(8,128)S(1)} %get-tuple-element.19), channel_id=1, source_target_pairs={{0,16},{8,24},{16,0},{24,8},{1,17},{9,25},{17,1},{25,9},{2,18},{10... | collective-permute-start | bytes 786440 | tf_op jit(solution)/shard_map/ppermute | solution.py:174
  83.1 11.9 %collective-permute-start.8 = (f32[128,512]{1,0:T(8,128)S(1)}, f32[128,512]{1,0:T(8,128)S(1)}, u32[]{:S(2)}, u32[]{:S(2)}) collective-permute-start(f32[128,512]{1,0:T(8,128)S(1)} %get-tuple-element.17), channel_id=1, source_target_pairs={{0,8},{8,0},{16,24},{24,16},{1,9},{9,1},{17,25},{25,17},{2,10},{10... | collective-permute-start | bytes 786440 | tf_op jit(solution)/shard_map/ppermute | solution.py:174

commit v2 on v0

v2 whole, which is shorter than its diff:
```python
import jax
import jax.numpy as jnp
from jax import lax
from jax.experimental import pallas as pl
from jax.experimental.pallas import tpu as pltpu
from jax.sharding import PartitionSpec as P

CHUNK = 16
LAG = 3
MESH = pl.DeviceIdType.MESH
BF16, F32 = jnp.bfloat16, jnp.float32


def kernel(
    groups, bands, scale, u_hbm, v_hbm, h_hbm, q_hbm, f_hbm, c_hbm, shift_ref, slope_ref, out_ref,
    u, v, h, q, f, c, dlon, anom, mean_rows, got, moment, parts,
    wind_sem, rest_sem, halo_send, halo_recv, mean_send, mean_recv, part_send, part_recv,
):
    members, extended, lons, levels = u.shape
    height = extended - 4
    share = lons // groups
    block = moment.shape[0] // groups
    me = lax.axis_index("member")
    band = lax.axis_index("space")
    has_low, has_high = band > 0, band < bands - 1
    even = lax.rem(band, 2) == 0

    def target(j):
        return lax.rem(me + j, groups)

    def wind_copies(r):
        return [
            pltpu.make_async_copy(u_hbm.at[:, r], u.at[:, r + 2], wind_sem.at[r, 0]),
            pltpu.make_async_copy(v_hbm.at[:, r], v.at[:, r + 2], wind_sem.at[r, 1]),
        ]

    def rest_copies(r):
        return [
            pltpu.make_async_copy(h_hbm.at[:, r], h.at[:, r], rest_sem.at[r, 0]),
            pltpu.make_async_copy(q_hbm.at[:, r], q.at[:, r], rest_sem.at[r, 1]),
            pltpu.make_async_copy(f_hbm.at[r], f.at[r], rest_sem.at[r, 2]),
            pltpu.make_async_copy(c_hbm.at[r], c.at[r], rest_sem.at[r, 3]),
        ]

    def halo_copies(up):
        here = height - 2 if up else 0
        there = 0 if up else height + 2
        to = band + 1 if up else band - 1
        return [
            pltpu.make_async_remote_copy(
                src_ref=src.at[:, pl.ds(here, 2)],
                dst_ref=dst.at[:, pl.ds(there, 2)],
                send_sem=halo_send.at[int(up), k],
                recv_sem=halo_recv.at[int(up), k],
                device_id={"space": to},
                device_id_type=MESH,
            )
            for k, (src, dst) in enumerate(((u_hbm, u), (v_hbm, v)))
        ]

    def mean_copy(j, k):
        at = pl.ds(pl.multiple_of(target(j) * share, share), share)
        return pltpu.make_async_remote_copy(
            src_ref=mean_rows.at[k, at],
            dst_ref=got.at[k, j - 1],
            send_sem=mean_send.at[k, j - 1],
            recv_sem=mean_recv.at[k, j - 1],
            device_id={"member": target(j)},
            device_id_type=MESH,
        )

    def part_copy(j):
        at = pl.ds(pl.multiple_of(target(j) * block, block), block)
        return pltpu.make_async_remote_copy(
            src_ref=moment.at[at],
            dst_ref=parts.at[j - 1],
            send_sem=part_send.at[j - 1],
            recv_sem=part_recv.at[j - 1],
            device_id={"member": target(j)},
            device_id_type=MESH,
        )

    def row_of(k):
        first = jnp.where(even, height - 2, 0)
        second = jnp.where(even, 0, height - 2)
        inner = height - 4
        return jnp.where(k < inner, k + 2, jnp.where(k < inner + 2, first + k - inner, second + k - inner - 2))

    barrier = pltpu.get_barrier_semaphore()
    for j in range(1, groups):
        pl.semaphore_signal(barrier, inc=1, device_id={"member": target(j)}, device_id_type=MESH)

    @pl.when(has_low)
    def _():
        pl.semaphore_signal(barrier, inc=1, device_id={"space": band - 1}, device_id_type=MESH)

    @pl.when(has_high)
    def _():
        pl.semaphore_signal(barrier, inc=1, device_id={"space": band + 1}, device_id_type=MESH)

    def start_row(r, carry):
        for copy in wind_copies(r):
            copy.start()
        return carry

    def start_rest(k, carry):
        for copy in rest_copies(row_of(k)):
            copy.start()
        return carry

    lax.fori_loop(0, 5, start_row, 0)
    lax.fori_loop(0, 1, start_rest, 0)

    pl.semaphore_wait(barrier, groups - 1 + has_low.astype(jnp.int32) + has_high.astype(jnp.int32))

    @pl.when(has_low)
    def _():
        for copy in halo_copies(False):
            copy.start()

    @pl.when(has_high)
    def _():
        for copy in halo_copies(True):
            copy.start()

    lax.fori_loop(5, height, start_row, 0)
    lax.fori_loop(1, height, start_rest, 0)

    moment[...] = jnp.zeros_like(moment)

    @pl.when(jnp.logical_not(has_low))
    def _():
        u[:, pl.ds(0, 2)] = jnp.zeros((members, 2, lons, levels), BF16)
        v[:, pl.ds(0, 2)] = jnp.zeros((members, 2, lons, levels), BF16)

    @pl.when(jnp.logical_not(has_high))
    def _():
        u[:, pl.ds(height + 2, 2)] = jnp.zeros((members, 2, lons, levels), BF16)
        v[:, pl.ds(height + 2, 2)] = jnp.zeros((members, 2, lons, levels), BF16)

    def receive_low():
        for copy in halo_copies(True):
            copy.wait_recv()

    def receive_high():
        for copy in halo_copies(False):
            copy.wait_recv()

    def wait_row(r, carry):
        for copy in wind_copies(r):
            copy.wait()
        return carry

    lax.fori_loop(0, 4, wait_row, 0)

    def between(k, carry):
        for j in range(1, groups):
            mean_copy(j, k).wait_recv()
        at = pl.ds(pl.multiple_of(me * share, share), share)
        each = [mean_rows[k, at].astype(F32)]
        each += [got[k, j].astype(F32) for j in range(groups - 1)]
        mean = sum(each[1:], each[0]) * (1.0 / groups)
        away = jnp.concatenate([a - mean for a in each], axis=0).astype(BF16)
        moment[...] += members * lax.dot_general(
            away, away, (((0,), (0,)), ((), ())), preferred_element_type=F32
        )
        return carry

    def row(k, carry):
        r = row_of(k)
        e = r + 2
        inner = height - 4

        @pl.when(k < inner)
        def _():
            wait_row(k + 4, 0)

        @pl.when((k == inner) & even & has_high | (k == inner + 2) & jnp.logical_not(even) & has_high)
        def _():
            receive_high()

        @pl.when((k == inner + 2) & even & has_low | (k == inner) & jnp.logical_not(even) & has_low)
        def _():
            receive_low()

        for copy in rest_copies(r):
            copy.wait()
        for m in range(members):
            both = jnp.concatenate([v[m, e], u[m, e]], axis=1)
            dlon[m] = jnp.dot(shift_ref[...], both, preferred_element_type=F32)

        def chunk(i, carry):
            at = pl.ds(pl.multiple_of(i * CHUNK, CHUNK), CHUNK)
            factor = f[r, at, :]
            curl_factor = c[r, at, :]
            slope = slope_ref[...]
            held, total = [], None
            for m in range(members):

                def wind(ref, d):
                    return ref[m, e + d, at, :].astype(F32)

                def lat(ref):
                    return 8.0 * (wind(ref, 1) - wind(ref, -1)) - (wind(ref, 2) - wind(ref, -2))

                curl = factor * (dlon[m, at, :levels] - lat(u))
                spread = factor * (dlon[m, at, levels:] + lat(v))
                heat = h[m, r, at, :].astype(F32) - curl_factor * curl
                moist = q[m, r, at, :].astype(F32) - slope * heat
                state = (curl, spread, heat, moist)
                held.append(state)
                total = state if total is None else tuple(a + b for a, b in zip(total, state))
            mean = tuple(a * (1.0 / members) for a in total)
            for n in range(4):
                lanes = slice(n * levels, (n + 1) * levels)
                mean_rows[k, at, lanes] = mean[n].astype(BF16)
                for m in range(members):
                    to = pl.ds(pl.multiple_of(m * lons + i * CHUNK, CHUNK), CHUNK)
                    anom[to, lanes] = (held[m][n] - mean[n]).astype(BF16)
            return carry

        lax.fori_loop(0, lons // CHUNK, chunk, 0)
        for j in range(1, groups):
            mean_copy(j, k).start()
        a = anom[...]
        moment[...] += lax.dot_general(a, a, (((0,), (0,)), ((), ())), preferred_element_type=F32)

        @pl.when(k >= LAG)
        def _():
            between(k - LAG, 0)

        return carry

    lax.fori_loop(0, height, row, 0)
    lax.fori_loop(height - LAG, height, between, 0)
    for j in range(1, groups):
        part_copy(j).start()
    total = moment[pl.ds(pl.multiple_of(me * block, block), block), :]
    for j in range(1, groups):
        part_copy(j).wait_recv()
        total += parts[j - 1]
    out_ref[...] = total * scale

    def sent(k, carry):
        for j in range(1, groups):
            mean_copy(j, k).wait_send()
        return carry

    lax.fori_loop(0, height, sent, 0)
    for j in range(1, groups):
        part_copy(j).wait_send()

    @pl.when(has_low)
    def _():
        for copy in halo_copies(False):
            copy.wait_send()

    @pl.when(has_high)
    def _():
        for copy in halo_copies(True):
            copy.wait_send()


def on_device(u, v, h, q, projection_scale, balance_multiplier, heat_slope, moist_slope):
    members, height, lons, levels = u.shape
    groups = lax.axis_size("member")
    bands = lax.axis_size("space")
    width = 4 * levels
    scale = 1.0 / ((members * groups - 1) * height * lons)
    shape = (height, lons, levels)
    factor = jnp.broadcast_to((projection_scale / 12.0)[:, :, None], shape)
    curl_factor = balance_multiplier[:, :, None] * heat_slope
    j = lax.broadcasted_iota(jnp.int32, (lons, lons), 0)
    i = lax.broadcasted_iota(jnp.int32, (lons, lons), 1)
    ahead = lax.rem(i - j + lons, lons)
    shift = jnp.where(ahead == 1, 6.0, jnp.where(ahead == lons - 1, -6.0, 0.0)).astype(BF16)
    slope = moist_slope[None]
    share, block, others = lons // groups, width // groups, groups - 1
    hbm = pl.BlockSpec(memory_space=pl.ANY)
    vmem = pl.BlockSpec(memory_space=pltpu.VMEM)
    dma = pltpu.SemaphoreType.DMA

    def body(*refs):
        kernel(groups, bands, scale, *refs)

    out = pl.pallas_call(
        body,
        out_shape=jax.ShapeDtypeStruct((block, width), F32),
        in_specs=[hbm] * 6 + [vmem] * 2,
        out_specs=vmem,
        scratch_shapes=[
            pltpu.VMEM((members, height + 4, lons, levels), BF16),
            pltpu.VMEM((members, height + 4, lons, levels), BF16),
            pltpu.VMEM((members, height, lons, levels), BF16),
            pltpu.VMEM((members, height, lons, levels), BF16),
            pltpu.VMEM(shape, F32),
            pltpu.VMEM(shape, F32),
            pltpu.VMEM((members, lons, 2 * levels), F32),
            pltpu.VMEM((members * lons, width), BF16),
            pltpu.VMEM((height, lons, width), BF16),
            pltpu.VMEM((height, others, share, width), BF16),
            pltpu.VMEM((width, width), F32),
            pltpu.VMEM((others, block, width), F32),
            dma((height, 2)),
            dma((height, 4)),
            dma((2, 2)),
            dma((2, 2)),
            dma((height, others)),
            dma((height, others)),
            dma((others,)),
            dma((others,)),
        ],
        compiler_params=pltpu.CompilerParams(
            collective_id=0, has_side_effects=True, vmem_limit_bytes=56 * 2**20
        ),
        cost_estimate=pl.CostEstimate(
            flops=2 * members * height * lons * width * width,
            bytes_accessed=16 * 2**20,
            transcendentals=0,
        ),
        name="band_moments",
    )(u, v, h, q, factor, curl_factor, shift, slope)
    return out[None]


def solution(mesh):
    placed = (
        P("member", "space", None, None),
        P("member", "space", None, None),
        P("member", "space", None, None),
        P("member", "space", None, None),
        P("space", None),
        P("space", None),
        P(),
        P(),
    )
    return jax.shard_map(
        on_device, mesh=mesh, in_specs=placed, out_specs=P("space", "member", None), check_vma=False
    )
```

time: 298 us -> 55.1 us (0.18)
  waiting for transfers between devices: 144 us -> 0 us
  other arithmetic: 69.9 us -> 3.51 us
  Pallas kernels: 0 us -> 48.4 us
  matrix products: 47.7 us -> 0 us
  local copies, waits for them, and re-layouts: 18.8 us -> 3 us
  between operations: 13.5 us -> 0.01 us
  starting transfers between devices: 4.11 us -> 0 us
    psum x2 -> x0, waiting for transfers between devices: 139 us -> none  [the longest x1 86.4 us: on_device(): lax.psum(local_sum.astype(jnp.bfloat16), 'member').astype(jnp.float32)]
    pallas_call x0 -> x1, Pallas kernels: none -> 48.4 us  [on_device(): pl.pallas_call(body, out_shape=jax.ShapeDtypeStruct((block, width), F32),...]
    dot_general x1 -> x0, matrix products: 47.7 us -> none  [gram_rows(): lax.dot_general(left, right, (((0,), (0,)), ((), ())), preferred_element_...]
    another operation x2 -> x0, other arithmetic: 37 us -> none
    slice x2 -> x0, local copies, waits for them, and re-layouts: 17 us -> none  [lon_diff(): return (jnp.roll(field, -1, 2) - jnp.roll(field, 1, 2)) / 2.0]
    convert_element_type x1, other arithmetic: 12.8 us -> 0.73 us  [on_device(): jnp.where(ahead == 1, 6.0, jnp.where(ahead == lons - 1, -6.0, 0.0))]
    reduce_sum x1 -> x0, other arithmetic: 8.08 us -> none  [on_device(): local_sum = jnp.sum(sample_vector.astype(jnp.float32), axis=0)]
    ppermute x2 -> x0, waiting for transfers between devices: 4.73 us -> none  [the longest x1 4.48 us: extended(): lax.ppermute(lax.slice_in_dim(block, 0, width, axis=dim), axis, backward)]
  transfers between devices with their start and end apart: 4 -> 0, of which waited for: 4 -> 0; matrix products, arithmetic and copies ran while one was open for 0% -> 0% of each run, Pallas kernels for 0% -> 0%
where the time goes in v2:
time: 55.1 us; the launch traced here: 54.9 us
  Pallas kernels  48.4 us (88%)
  other arithmetic  3.51 us (6%)
  local copies, waits for them, and re-layouts  3 us (5%)
    pallas_call x1, Pallas kernels, on_device(): pl.pallas_call(body, out_shape=jax.ShapeDtypeStruct((block, width), F32),...  48.4 us
    mul x1, other arithmetic, on_device(): curl_factor = balance_multiplier[:, :, None] * heat_slope  2.08 us
    unnamed x1, local copies, waits for them, and re-layouts  1.67 us
    broadcast_in_dim x1, local copies, waits for them, and re-layouts, on_device(): factor = jnp.broadcast_to((projection_scale / 12.0)[:, :, None], shape)  1.32 us

profile of v2, /device:TPU:0, one launch (start us, length us, event | category | flops | bytes accessed | tf_op | source)
XLA Modules:
  0.0 54.9 jit_solution(13545803548153061694)
XLA Ops:
  0.0 0.7 %broadcast_multiply_fusion.1 = f32[8,256]{1,0:T(8,128)S(1)} fusion(f32[8,256]{1,0:T(8,128)} %param.12), kind=kLoop, calls=%fused_computation.5 | loop fusion | flops 2048 | bytes 16384 | tf_op jit(solution)/shard_map/div | solution.py:271
  0.7 0.7 %select_convert_fusion.refs_6_ = bf16[256,256]{1,0:T(8,128)(2,1)} fusion(), kind=kLoop, calls=%fused_computation.4 | loop fusion | flops 851968 | bytes 131072 | tf_op jit(solution)/shard_map/convert_element_type | solution.py:276
  1.4 1.3 %broadcast_in_dim.26.refs_4_ = f32[8,256,128]{2,1,0:T(8,128)} broadcast(f32[8,256]{1,0:T(8,128)S(1)} %broadcast_multiply_fusion.1), dimensions={0,1} | broadcast | bytes 1056768 | tf_op jit(solution)/shard_map/broadcast_in_dim | solution.py:271
  2.8 2.1 %broadcast_multiply_fusion.refs_5_ = f32[8,256,128]{2,1,0:T(8,128)} fusion(f32[128]{0:T(128)} %param.14, f32[8,256]{1,0:T(8,128)} %param.13), kind=kLoop, calls=%fused_computation | loop fusion | flops 262144 | bytes 1057280 | tf_op jit(solution)/shard_map/mul | solution.py:272
  4.8 48.4 %band_moments.1 = f32[128,512]{1,0:T(8,128)} custom-call(bf16[6,8,256,128]{3,2,1,0:T(8,128)(2,1)} %refs_0_.1, bf16[6,8,256,128]{3,2,1,0:T(8,128)(2,1)} %refs_1_.1, bf16[6,8,256,128]{3,2,1,0:T(8,128)(2,1)} %refs_2_.1, bf16[6,8,256,128]{3,2,1,0:T(8,128)(2,1)} %refs_3_.1, f32[8,256,128]{2,1,0:T(8,128)} %broadcast_in_dim.26.refs_4_, ...), custom_call_target="tpu_custom_call" | custom-call | flops 6442450944 | bytes 16777216 | tf_op jit(solution)/shard_map/band_moments/pallas_call | solution.py:286
  53.2 1.7 %copy.10 = f32[1,128,512]{2,1,0:T(8,128)} copy(f32[1,128,512]{2,1,0:T(8,128)} %bitcast.2) | data formatting | bytes 524288

commit v3 on v2

--- a/solution.py
+++ b/solution.py
@@ -1,3 +1,5 @@
+import functools
+
 import jax
 import jax.numpy as jnp
 from jax import lax
@@ -12,12 +14,13 @@
 
 
 def kernel(
-    groups, bands, scale, u_hbm, v_hbm, h_hbm, q_hbm, f_hbm, c_hbm, shift_ref, slope_ref, out_ref,
-    u, v, h, q, f, c, dlon, anom, mean_rows, got, moment, parts,
+    groups, bands, u_hbm, v_hbm, h_hbm, q_hbm, scale_ref, balance_ref, heat_slope_ref, slope_ref, out_ref,
+    u, v, h, q, f, c, shift, dlon_a, dlon_b, anom_a, anom_b, mean_rows, got, moment, parts,
     wind_sem, rest_sem, halo_send, halo_recv, mean_send, mean_recv, part_send, part_recv,
 ):
     members, extended, lons, levels = u.shape
     height = extended - 4
+    half = lons // 2
     share = lons // groups
     block = moment.shape[0] // groups
     me = lax.axis_index("member")
@@ -38,8 +41,6 @@
         return [
             pltpu.make_async_copy(h_hbm.at[:, r], h.at[:, r], rest_sem.at[r, 0]),
             pltpu.make_async_copy(q_hbm.at[:, r], q.at[:, r], rest_sem.at[r, 1]),
-            pltpu.make_async_copy(f_hbm.at[r], f.at[r], rest_sem.at[r, 2]),
-            pltpu.make_async_copy(c_hbm.at[r], c.at[r], rest_sem.at[r, 3]),
         ]
 
     def halo_copies(up):
@@ -127,6 +128,23 @@
     lax.fori_loop(1, height, start_rest, 0)
 
     moment[...] = jnp.zeros_like(moment)
+    anom_b[...] = jnp.zeros_like(anom_b)
+    here = lax.broadcasted_iota(jnp.int32, (lons, lons), 0)
+    there = lax.broadcasted_iota(jnp.int32, (lons, lons), 1)
+    ahead = there - here
+    right = (ahead == 1) | (ahead == 1 - lons)
+    left = (ahead == -1) | (ahead == lons - 1)
+    shift[...] = jnp.where(right, 6.0, jnp.where(left, -6.0, 0.0)).astype(BF16)
+
+    def factors(r, carry):
+        def spread(ref):
+            return jnp.broadcast_to(ref[pl.ds(r, 1), :], (levels, lons)).T
+
+        f[r] = spread(scale_ref) * (1.0 / 12.0)
+        c[r] = spread(balance_ref) * heat_slope_ref[...]
+        return carry
+
+    lax.fori_loop(0, height, factors, 0)
 
     @pl.when(jnp.logical_not(has_low))
     def _():
@@ -152,6 +170,23 @@
         return carry
 
     lax.fori_loop(0, 4, wait_row, 0)
+
+    def gram(a, times):
+        cut = a.shape[1] // 2
+        top = lax.dot_general(
+            a[:, :cut], a, (((0,), (0,)), ((), ())), preferred_element_type=F32
+        )
+        low = lax.dot_general(
+            a[:, cut:], a[:, cut:], (((0,), (0,)), ((), ())), preferred_element_type=F32
+        )
+        moment[:cut, :] += top if times == 1 else times * top
+        moment[cut:, cut:] += low if times == 1 else times * low
+
+    def longitude(dlon, e, side):
+        at = slice(side * half, (side + 1) * half)
+        for m in range(members):
+            both = jnp.concatenate([v[m, e], u[m, e]], axis=1)
+            dlon[m] = jnp.dot(shift[at, :], both, preferred_element_type=F32)
 
     def between(k, carry):
         for j in range(1, groups):
@@ -161,9 +196,7 @@
         each += [got[k, j].astype(F32) for j in range(groups - 1)]
         mean = sum(each[1:], each[0]) * (1.0 / groups)
         away = jnp.concatenate([a - mean for a in each], axis=0).astype(BF16)
-        moment[...] += members * lax.dot_general(
-            away, away, (((0,), (0,)), ((), ())), preferred_element_type=F32
-        )
+        gram(away, members)
         return carry
 
     def row(k, carry):
@@ -185,12 +218,9 @@
 
         for copy in rest_copies(r):
             copy.wait()
-        for m in range(members):
-            both = jnp.concatenate([v[m, e], u[m, e]], axis=1)
-            dlon[m] = jnp.dot(shift_ref[...], both, preferred_element_type=F32)
-
-        def chunk(i, carry):
-            at = pl.ds(pl.multiple_of(i * CHUNK, CHUNK), CHUNK)
+        def chunk(side, dlon, anom, i, carry):
+            within = pl.ds(pl.multiple_of(i * CHUNK, CHUNK), CHUNK)
+            at = pl.ds(pl.multiple_of(side * half + i * CHUNK, CHUNK), CHUNK)
             factor = f[r, at, :]
             curl_factor = c[r, at, :]
             slope = slope_ref[...]
@@ -203,8 +233,8 @@
                 def lat(ref):
                     return 8.0 * (wind(ref, 1) - wind(ref, -1)) - (wind(ref, 2) - wind(ref, -2))
 
-                curl = factor * (dlon[m, at, :levels] - lat(u))
-                spread = factor * (dlon[m, at, levels:] + lat(v))
+                curl = factor * (dlon[m, within, :levels] - lat(u))
+                spread = factor * (dlon[m, within, levels:] + lat(v))
                 heat = h[m, r, at, :].astype(F32) - curl_factor * curl
                 moist = q[m, r, at, :].astype(F32) - slope * heat
                 state = (curl, spread, heat, moist)
@@ -215,15 +245,19 @@
                 lanes = slice(n * levels, (n + 1) * levels)
                 mean_rows[k, at, lanes] = mean[n].astype(BF16)
                 for m in range(members):
-                    to = pl.ds(pl.multiple_of(m * lons + i * CHUNK, CHUNK), CHUNK)
+                    to = pl.ds(pl.multiple_of(m * half + i * CHUNK, CHUNK), CHUNK)
                     anom[to, lanes] = (held[m][n] - mean[n]).astype(BF16)
             return carry
 
-        lax.fori_loop(0, lons // CHUNK, chunk, 0)
+        steps = half // CHUNK
+        gram(anom_b[...], 1)
+        longitude(dlon_b, e, 1)
+        lax.fori_loop(0, steps, functools.partial(chunk, 0, dlon_a, anom_a), 0, unroll=True)
+        gram(anom_a[...], 1)
+        longitude(dlon_a, row_of(jnp.minimum(k + 1, height - 1)) + 2, 0)
+        lax.fori_loop(0, steps, functools.partial(chunk, 1, dlon_b, anom_b), 0, unroll=True)
         for j in range(1, groups):
             mean_copy(j, k).start()
-        a = anom[...]
-        moment[...] += lax.dot_general(a, a, (((0,), (0,)), ((), ())), preferred_element_type=F32)
 
         @pl.when(k >= LAG)
         def _():
@@ -231,15 +265,19 @@
 
         return carry
 
+    longitude(dlon_a, row_of(0) + 2, 0)
     lax.fori_loop(0, height, row, 0)
+    gram(anom_b[...], 1)
     lax.fori_loop(height - LAG, height, between, 0)
+    cut = moment.shape[0] // 2
+    moment[cut:, :cut] = moment[:cut, cut:].T
     for j in range(1, groups):
         part_copy(j).start()
     total = moment[pl.ds(pl.multiple_of(me * block, block), block), :]
     for j in range(1, groups):
         part_copy(j).wait_recv()
         total += parts[j - 1]
-    out_ref[...] = total * scale
+    out_ref[...] = total
 
     def sent(k, carry):
         for j in range(1, groups):
@@ -268,25 +306,18 @@
     width = 4 * levels
     scale = 1.0 / ((members * groups - 1) * height * lons)
     shape = (height, lons, levels)
-    factor = jnp.broadcast_to((projection_scale / 12.0)[:, :, None], shape)
-    curl_factor = balance_multiplier[:, :, None] * heat_slope
-    j = lax.broadcasted_iota(jnp.int32, (lons, lons), 0)
-    i = lax.broadcasted_iota(jnp.int32, (lons, lons), 1)
-    ahead = lax.rem(i - j + lons, lons)
-    shift = jnp.where(ahead == 1, 6.0, jnp.where(ahead == lons - 1, -6.0, 0.0)).astype(BF16)
-    slope = moist_slope[None]
     share, block, others = lons // groups, width // groups, groups - 1
     hbm = pl.BlockSpec(memory_space=pl.ANY)
     vmem = pl.BlockSpec(memory_space=pltpu.VMEM)
     dma = pltpu.SemaphoreType.DMA
 
     def body(*refs):
-        kernel(groups, bands, scale, *refs)
+        kernel(groups, bands, *refs)
 
     out = pl.pallas_call(
         body,
         out_shape=jax.ShapeDtypeStruct((block, width), F32),
-        in_specs=[hbm] * 6 + [vmem] * 2,
+        in_specs=[hbm] * 4 + [vmem] * 4,
         out_specs=vmem,
         scratch_shapes=[
             pltpu.VMEM((members, height + 4, lons, levels), BF16),
@@ -295,14 +326,17 @@
             pltpu.VMEM((members, height, lons, levels), BF16),
             pltpu.VMEM(shape, F32),
             pltpu.VMEM(shape, F32),
-            pltpu.VMEM((members, lons, 2 * levels), F32),
-            pltpu.VMEM((members * lons, width), BF16),
+            pltpu.VMEM((lons, lons), BF16),
+            pltpu.VMEM((members, lons // 2, 2 * levels), F32),
+            pltpu.VMEM((members, lons // 2, 2 * levels), F32),
+            pltpu.VMEM((members * lons // 2, width), BF16),
+            pltpu.VMEM((members * lons // 2, width), BF16),
             pltpu.VMEM((height, lons, width), BF16),
             pltpu.VMEM((height, others, share, width), BF16),
             pltpu.VMEM((width, width), F32),
             pltpu.VMEM((others, block, width), F32),
             dma((height, 2)),
-            dma((height, 4)),
+            dma((height, 2)),
             dma((2, 2)),
             dma((2, 2)),
             dma((height, others)),
@@ -319,8 +353,8 @@
             transcendentals=0,
         ),
         name="band_moments",
-    )(u, v, h, q, factor, curl_factor, shift, slope)
-    return out[None]
+    )(u, v, h, q, projection_scale, balance_multiplier, heat_slope[None], moist_slope[None])
+    return (out * scale)[None]
 
 
 def solution(mesh):

time: 55.1 us -> 49.2 us (0.89)
  the two profiles are of different devices: /device:TPU:0 before, /device:TPU:9 now
where the time goes in v3:
time: 49.2 us; the launch traced here: 49 us
  Pallas kernels  47.3 us (96%)
  other arithmetic  1.68 us (3%)
    pallas_call x1, Pallas kernels, on_device(): pl.pallas_call(body, out_shape=jax.ShapeDtypeStruct((block, width), F32),...  47.3 us
    broadcast_in_dim x1, other arithmetic, on_device(): return (out * scale)[None]  1.68 us

profile of v3, /device:TPU:9, one launch (start us, length us, event | category | flops | bytes accessed | tf_op | source)
XLA Modules:
  0.0 49.0 jit_solution(6502212912154734029)
XLA Ops:
  0.0 47.3 %band_moments.1 = f32[128,512]{1,0:T(8,128)} custom-call(bf16[6,8,256,128]{3,2,1,0:T(8,128)(2,1)} %refs_0_.1, bf16[6,8,256,128]{3,2,1,0:T(8,128)(2,1)} %refs_1_.1, bf16[6,8,256,128]{3,2,1,0:T(8,128)(2,1)} %refs_2_.1, bf16[6,8,256,128]{3,2,1,0:T(8,128)(2,1)} %refs_3_.1, f32[8,256]{1,0:T(8,128)} %refs_4_.1, f32[8,256]{1,0:T(8,128)} %refs_5_.1, ...), custom_call_target="tpu_custom_call" | custom-call | flops 6442450944 | bytes 16777216 | tf_op jit(solution)/shard_map/band_moments/pallas_call | solution.py:317
  47.3 1.7 %multiply_bitcast_fusion = f32[1,128,512]{2,1,0:T(8,128)} fusion(f32[128,512]{1,0:T(8,128)} %band_moments.1), kind=kLoop, calls=%fused_computation | loop fusion | flops 65536 | bytes 524288 | tf_op jit(solution)/shard_map/broadcast_in_dim | solution.py:357

commit v4 on v3

--- a/solution.py
+++ b/solution.py
@@ -1,4 +1,5 @@
 import functools
+import itertools
 
 import jax
 import jax.numpy as jnp
@@ -8,28 +9,35 @@
 from jax.sharding import PartitionSpec as P
 
 CHUNK = 16
-LAG = 3
 MESH = pl.DeviceIdType.MESH
 BF16, F32 = jnp.bfloat16, jnp.float32
 
 
 def kernel(
     groups, bands, u_hbm, v_hbm, h_hbm, q_hbm, scale_ref, balance_ref, heat_slope_ref, slope_ref, out_ref,
-    u, v, h, q, f, c, shift, dlon_a, dlon_b, anom_a, anom_b, mean_rows, got, moment, parts,
+    u, v, h, q, f, c, shift, dlon_a, dlon_b, anom_a, anom_b, mean_rows, got, kept, away, moment, parts,
     wind_sem, rest_sem, halo_send, halo_recv, mean_send, mean_recv, part_send, part_recv,
 ):
     members, extended, lons, levels = u.shape
     height = extended - 4
     half = lons // 2
-    share = lons // groups
-    block = moment.shape[0] // groups
+    width = moment.shape[1]
+    block = width // groups
+    bits = groups.bit_length() - 1
+    orders = (tuple(range(bits)), tuple(reversed(range(bits))))
+    columns = width // 2
+    sizes = [lons // 2 ** (t + 2) for t in range(bits)]
+    starts = [2 * sum(sizes[:t]) for t in range(bits)]
     me = lax.axis_index("member")
     band = lax.axis_index("space")
     has_low, has_high = band > 0, band < bands - 1
     even = lax.rem(band, 2) == 0
 
-    def target(j):
-        return lax.rem(me + j, groups)
+    def bit(b):
+        return lax.rem(lax.div(me, 2**b), 2)
+
+    def partner(b):
+        return me + (1 - 2 * bit(b)) * 2**b
 
     def wind_copies(r):
         return [
@@ -59,27 +67,57 @@
             for k, (src, dst) in enumerate(((u_hbm, u), (v_hbm, v)))
         ]
 
-    def mean_copy(j, k):
-        at = pl.ds(pl.multiple_of(target(j) * share, share), share)
+    def piece(t, stream, k, keep):
+        b = bit(orders[stream][t])
+        b = b if keep else 1 - b
+        size = sizes[t]
+        if t == 0:
+            at = pl.multiple_of(stream * half + b * size, size)
+            return mean_rows.at[k, pl.ds(at, size)]
+        at = pl.multiple_of(starts[t - 1] + stream * sizes[t - 1] + b * size, size)
+        return kept.at[k, pl.ds(at, size)]
+
+    def mean_copy(t, stream, k):
         return pltpu.make_async_remote_copy(
-            src_ref=mean_rows.at[k, at],
-            dst_ref=got.at[k, j - 1],
-            send_sem=mean_send.at[k, j - 1],
-            recv_sem=mean_recv.at[k, j - 1],
-            device_id={"member": target(j)},
+            src_ref=piece(t, stream, k, False),
+            dst_ref=got.at[k, pl.ds(starts[t] + stream * sizes[t], sizes[t])],
+            send_sem=mean_send.at[k, t, stream],
+            recv_sem=mean_recv.at[k, t, stream],
+            device_id={"member": partner(orders[stream][t])},
             device_id_type=MESH,
         )
 
-    def part_copy(j):
-        at = pl.ds(pl.multiple_of(target(j) * block, block), block)
+    def flips(t):
+        return list(itertools.product((1, 0), repeat=bits - 1 - t))
+
+    def part_view(t, stream, flip, keep):
+        order = orders[stream]
+        owner = 0
+        for place, b in enumerate(order):
+            other = (not keep) if place == t else place > t and flip[place - t - 1]
+            owner = owner + (1 - bit(b) if other else bit(b)) * 2**b
+        return moment.at[
+            pl.ds(pl.multiple_of(owner * block, block), block), pl.ds(stream * columns, columns)
+        ]
+
+    def slot(t, flip):
+        return sum(2 ** (bits - 1 - x) for x in range(t)) + flips(t).index(flip)
+
+    def part_copy(t, stream, flip):
+        n = slot(t, flip)
         return pltpu.make_async_remote_copy(
-            src_ref=moment.at[at],
-            dst_ref=parts.at[j - 1],
-            send_sem=part_send.at[j - 1],
-            recv_sem=part_recv.at[j - 1],
-            device_id={"member": target(j)},
+            src_ref=part_view(t, stream, flip, False),
+            dst_ref=parts.at[stream, n],
+            send_sem=part_send.at[stream, n],
+            recv_sem=part_recv.at[stream, n],
+            device_id={"member": partner(orders[stream][t])},
             device_id_type=MESH,
         )
+
+    def take(t, stream, flip):
+        part_copy(t, stream, flip).wait_recv()
+        view = part_view(t, stream, flip, True)
+        view[...] += parts[stream, slot(t, flip)]
 
     def row_of(k):
         first = jnp.where(even, height - 2, 0)
@@ -88,8 +126,8 @@
         return jnp.where(k < inner, k + 2, jnp.where(k < inner + 2, first + k - inner, second + k - inner - 2))
 
     barrier = pltpu.get_barrier_semaphore()
-    for j in range(1, groups):
-        pl.semaphore_signal(barrier, inc=1, device_id={"member": target(j)}, device_id_type=MESH)
+    for b in range(bits):
+        pl.semaphore_signal(barrier, inc=1, device_id={"member": partner(b)}, device_id_type=MESH)
 
     @pl.when(has_low)
     def _():
@@ -112,7 +150,7 @@
     lax.fori_loop(0, 5, start_row, 0)
     lax.fori_loop(0, 1, start_rest, 0)
 
-    pl.semaphore_wait(barrier, groups - 1 + has_low.astype(jnp.int32) + has_high.astype(jnp.int32))
+    pl.semaphore_wait(barrier, bits + has_low.astype(jnp.int32) + has_high.astype(jnp.int32))
 
     @pl.when(has_low)
     def _():
@@ -188,16 +226,19 @@
             both = jnp.concatenate([v[m, e], u[m, e]], axis=1)
             dlon[m] = jnp.dot(shift[at, :], both, preferred_element_type=F32)
 
-    def between(k, carry):
-        for j in range(1, groups):
-            mean_copy(j, k).wait_recv()
-        at = pl.ds(pl.multiple_of(me * share, share), share)
-        each = [mean_rows[k, at].astype(F32)]
-        each += [got[k, j].astype(F32) for j in range(groups - 1)]
-        mean = sum(each[1:], each[0]) * (1.0 / groups)
-        away = jnp.concatenate([a - mean for a in each], axis=0).astype(BF16)
-        gram(away, members)
-        return carry
+    def merge(t, k):
+        for stream in range(2):
+            mean_copy(t, stream, k).wait_recv()
+            first = starts[t] + stream * sizes[t]
+            at = slice(first, first + sizes[t])
+            mine = piece(t, stream, k, True)[...].astype(F32)
+            theirs = got[k, at].astype(F32)
+            away[k, at] = ((mine - theirs) * 2.0 ** (t / 2)).astype(BF16)
+            if t + 1 < bits:
+                kept[k, at] = (0.5 * (mine + theirs)).astype(BF16)
+                mean_copy(t + 1, stream, k).start()
+        if t + 1 == bits:
+            gram(away[k], 0.5 * members)
 
     def row(k, carry):
         r = row_of(k)
@@ -256,37 +297,53 @@
         gram(anom_a[...], 1)
         longitude(dlon_a, row_of(jnp.minimum(k + 1, height - 1)) + 2, 0)
         lax.fori_loop(0, steps, functools.partial(chunk, 1, dlon_b, anom_b), 0, unroll=True)
-        for j in range(1, groups):
-            mean_copy(j, k).start()
-
-        @pl.when(k >= LAG)
-        def _():
-            between(k - LAG, 0)
+        for stream in range(2):
+            mean_copy(0, stream, k).start()
+        for t in range(bits):
+
+            @pl.when(k > t)
+            def _():
+                merge(t, k - t - 1)
 
         return carry
 
     longitude(dlon_a, row_of(0) + 2, 0)
     lax.fori_loop(0, height, row, 0)
     gram(anom_b[...], 1)
-    lax.fori_loop(height - LAG, height, between, 0)
+    for k in range(height, height + bits):
+        for t in range(bits):
+            if k - t - 1 < height:
+                merge(t, k - t - 1)
     cut = moment.shape[0] // 2
     moment[cut:, :cut] = moment[:cut, cut:].T
-    for j in range(1, groups):
-        part_copy(j).start()
-    total = moment[pl.ds(pl.multiple_of(me * block, block), block), :]
-    for j in range(1, groups):
-        part_copy(j).wait_recv()
-        total += parts[j - 1]
-    out_ref[...] = total
+    for flip in flips(0):
+        for stream in range(2):
+            part_copy(0, stream, flip).start()
+    for t in range(bits):
+        if t + 1 < bits:
+            for stream in range(2):
+                for flip in flips(t):
+                    if flip[0]:
+                        take(t, stream, flip)
+                for flip in flips(t + 1):
+                    part_copy(t + 1, stream, flip).start()
+        for stream in range(2):
+            for flip in flips(t):
+                if t + 1 == bits or not flip[0]:
+                    take(t, stream, flip)
+    out_ref[...] = moment[pl.ds(pl.multiple_of(me * block, block), block), :]
 
     def sent(k, carry):
-        for j in range(1, groups):
-            mean_copy(j, k).wait_send()
+        for t in range(bits):
+            for stream in range(2):
+                mean_copy(t, stream, k).wait_send()
         return carry
 
     lax.fori_loop(0, height, sent, 0)
-    for j in range(1, groups):
-        part_copy(j).wait_send()
+    for t in range(bits):
+        for stream in range(2):
+            for flip in flips(t):
+                part_copy(t, stream, flip).wait_send()
 
     @pl.when(has_low)
     def _():
@@ -306,7 +363,9 @@
     width = 4 * levels
     scale = 1.0 / ((members * groups - 1) * height * lons)
     shape = (height, lons, levels)
-    share, block, others = lons // groups, width // groups, groups - 1
+    block, others = width // groups, groups - 1
+    bits = groups.bit_length() - 1
+    merged = lons - lons // groups
     hbm = pl.BlockSpec(memory_space=pl.ANY)
     vmem = pl.BlockSpec(memory_space=pltpu.VMEM)
     dma = pltpu.SemaphoreType.DMA
@@ -332,17 +391,19 @@
             pltpu.VMEM((members * lons // 2, width), BF16),
             pltpu.VMEM((members * lons // 2, width), BF16),
             pltpu.VMEM((height, lons, width), BF16),
-            pltpu.VMEM((height, others, share, width), BF16),
+            pltpu.VMEM((height, merged, width), BF16),
+            pltpu.VMEM((height, merged, width), BF16),
+            pltpu.VMEM((height, merged, width), BF16),
             pltpu.VMEM((width, width), F32),
-            pltpu.VMEM((others, block, width), F32),
+            pltpu.VMEM((2, others, block, width // 2), F32),
             dma((height, 2)),
             dma((height, 2)),
             dma((2, 2)),
             dma((2, 2)),
-            dma((height, others)),
-            dma((height, others)),
-            dma((others,)),
-            dma((others,)),
+            dma((height, bits, 2)),
+            dma((height, bits, 2)),
+            dma((2, others)),
+            dma((2, others)),
         ],
         compiler_params=pltpu.CompilerParams(
             collective_id=0, has_side_effects=True, vmem_limit_bytes=56 * 2**20

time: 49.2 us -> 47.9 us (0.974)
  the two profiles are of different devices: /device:TPU:9 before, /device:TPU:0 now
where the time goes in v4:
time: 47.9 us; the launch traced here: 47.6 us
  Pallas kernels  46 us (96%)
  other arithmetic  1.68 us (4%)
    pallas_call x1, Pallas kernels, on_device(): pl.pallas_call(body, out_shape=jax.ShapeDtypeStruct((block, width), F32),...  46 us
    broadcast_in_dim x1, other arithmetic, on_device(): return (out * scale)[None]  1.68 us

profile of v4, /device:TPU:0, one launch (start us, length us, event | category | flops | bytes accessed | tf_op | source)
XLA Modules:
  0.0 47.6 jit_solution(13337883847380517172)
XLA Ops:
  0.0 46.0 %band_moments.1 = f32[128,512]{1,0:T(8,128)} custom-call(bf16[6,8,256,128]{3,2,1,0:T(8,128)(2,1)} %refs_0_.1, bf16[6,8,256,128]{3,2,1,0:T(8,128)(2,1)} %refs_1_.1, bf16[6,8,256,128]{3,2,1,0:T(8,128)(2,1)} %refs_2_.1, bf16[6,8,256,128]{3,2,1,0:T(8,128)(2,1)} %refs_3_.1, f32[8,256]{1,0:T(8,128)} %refs_4_.1, f32[8,256]{1,0:T(8,128)} %refs_5_.1, ...), custom_call_target="tpu_custom_call" | custom-call | flops 6442450944 | bytes 16777216 | tf_op jit(solution)/shard_map/band_moments/pallas_call | solution.py:376
  46.0 1.7 %multiply_bitcast_fusion = f32[1,128,512]{2,1,0:T(8,128)} fusion(f32[128,512]{1,0:T(8,128)} %band_moments.1), kind=kLoop, calls=%fused_computation | loop fusion | flops 65536 | bytes 524288 | tf_op jit(solution)/shard_map/broadcast_in_dim | solution.py:418
